TPU v7x, 32 devices: a whole 2x2x4 slice. The times are simulated.
32 devices in a mesh: dp: 8 (over z, y), tensor: 4 (over x, core).
Axes of the slice: x: 2, y: 2, z: 4, core: 2. Of those that a mesh axis runs over, the one named last changes fastest.
Arguments:
- gradient: bfloat16 [8, 128, 8192], P('dp', None, 'tensor'), may hold values from -600 to 600
- momentum: float32 [8, 128, 8192], P('dp', None, 'tensor'), may hold values from -8 to 8
Outputs:
- new_momentum: float32 [8, 128, 8192], P('dp', None, 'tensor')
- update: float32 [128, 8192], P(None, 'tensor')
All inputs are finite; a program needn't handle non-finite values.
Results may differ from a plain program's by a relative error of at most 0.0003.
Values sent between devices are 32-bit elements; how exact they have to be, the bound alone decides.
A program may use at most 64 MiB of HBM per device.

v0:
```python
import jax
import jax.numpy as jnp
from jax import lax
from jax.sharding import PartitionSpec as P

COLS = 8192
ROWS = 128
BLOCK = 64
KEEP = 8


momentum_decay = 0.999


def low_basis():
    freq = jnp.arange(KEEP, dtype=jnp.float32)[:, None]
    place = jnp.arange(BLOCK, dtype=jnp.float32)[None, :]
    table = jnp.cos(jnp.pi * (2.0 * place + 1.0) * freq / (2.0 * BLOCK))
    factor = jnp.where(freq == 0.0, jnp.sqrt(1.0 / BLOCK), jnp.sqrt(2.0 / BLOCK)).astype(
        jnp.float32
    )
    return table * factor


def encode(field, basis):
    rows, cols = field.shape
    tiles = field.reshape(rows // BLOCK, BLOCK, cols // BLOCK, BLOCK)
    return jnp.einsum("ka,racb,lb->rkcl", basis, tiles, basis, precision=lax.Precision.HIGHEST)


def decode(coeffs, basis):
    nrb, keep_a, ncb, keep_b = coeffs.shape
    tiles = jnp.einsum("ka,rkcl,lb->racb", basis, coeffs, basis, precision=lax.Precision.HIGHEST)
    return tiles.reshape(nrb * BLOCK, ncb * BLOCK)


def body(gradient, momentum):
    basis = low_basis()
    accum = momentum_decay * momentum[0] + gradient[0].astype(jnp.float32)
    coeffs = encode(accum, basis)
    nrb, keep_a, ncb, keep_b = coeffs.shape
    new_momentum = (accum - decode(coeffs, basis))[None]
    flat = coeffs.reshape(nrb * KEEP, ncb * KEEP)
    total = lax.psum(flat, "dp")
    decoded = decode(total.reshape(nrb, KEEP, ncb, KEEP), basis)
    squares = lax.psum(jnp.sum(decoded * decoded), "tensor")
    scale = jnp.sqrt(squares / (ROWS * COLS) + 1e-06)
    return (new_momentum, decoded / scale)


def solution(mesh):
    placed = (P("dp", None, "tensor"), P("dp", None, "tensor"))
    return jax.shard_map(
        body,
        mesh=mesh,
        in_specs=placed,
        out_specs=(P("dp", None, "tensor"), P(None, "tensor")),
        check_vma=False,
    )
```

profile of v0, /device:TPU:0, one launch (start us, length us, event | category | flops | bytes accessed | tf_op | source)
XLA Modules:
  0.0 69.9 jit_solution(4129865418067948460)
XLA Ops:
  0.6 1.5 %convert_add_fusion = f32[1,128,2048]{2,1,0:T(8,128)S(1)} fusion(bf16[1,128,2048]{2,1,0:T(8,128)(2,1)} %param.2, f32[1,128,2048]{2,1,0:T(8,128)} %param.3), kind=kLoop, calls=%fused_computation.6 | loop fusion | flops 786432 | bytes 2621440 | tf_op jit(solution)/shard_map/add | solution.py:39
  2.2 0.8 %add.37 = f32[2,64,32,64]{3,2,1,0:T(8,128)S(1)} reshape(f32[1,128,2048]{2,1,0:T(8,128)S(1)} %convert_add_fusion) | data formatting | bytes 2097152 | tf_op jit(solution)/shard_map/add | solution.py:39
  3.0 2.4 %fusion = f32[2,32,64,8]{2,3,1,0:T(8,128)S(1)} fusion(f32[2,64,32,64]{3,2,1,0:T(8,128)S(1)} %add.37, f32[8]{0:T(128)S(1)} %compare_select_fusion, f32[64]{0:T(128)S(1)} %add_multiply_fusion), kind=kOutput, calls=%fused_computation | convolution fusion | flops 25167360 | bytes 1179936 | tf_op jit(solution)/shard_map/ka,racb,lb->rkcl/dot_general | solution.py:28
  5.4 1.1 %convolution_bitcast_fusion.1 = f32[2,8,32,8]{2,3,1,0:T(8,128)S(1)} fusion(f32[2,32,64,8]{2,3,1,0:T(8,128)S(1)} %fusion, f32[8]{0:T(128)S(1)} %compare_select_fusion, f32[64]{0:T(128)S(1)} %add_multiply_fusion), kind=kOutput, calls=%fused_computation.5 | convolution fusion | flops 3147264 | bytes 147744 | tf_op jit(solution)/shard_map/ka,racb,lb->rkcl/dot_general | solution.py:28
  6.6 0.7 fusion.8
  7.2 3.5 %convolution_bitcast_fusion = f32[2,64,32,64]{3,1,2,0:T(8,128)S(1)} fusion(f32[2,32,8,64]{3,1,2,0:T(8,128)S(1)} %fusion.8, f32[8]{0:T(128)S(1)} %compare_select_fusion, f32[64]{0:T(128)S(1)} %add_multiply_fusion), kind=kOutput, calls=%fused_computation.4 | convolution fusion | flops 25167360 | bytes 1179936 | tf_op jit(solution)/shard_map/ka,rkcl,lb->racb/dot_general | solution.py:33
  10.7 1.2 %copy.4 = f32[2,64,32,64]{3,2,1,0:T(8,128)S(1)} copy(f32[2,64,32,64]{3,1,2,0:T(8,128)S(1)} %convolution_bitcast_fusion) | data formatting | bytes 2097152 | tf_op jit(solution)/shard_map/ka,rkcl,lb->racb/transpose | solution.py:33
  11.9 1.6 %reshape.40 = f32[1,128,2048]{2,1,0:T(8,128)} reshape(f32[2,64,32,64]{3,2,1,0:T(8,128)S(1)} %copy.4) | data formatting | bytes 2097152 | tf_op jit(solution)/shard_map/reshape | solution.py:34
  13.6 2.3 %sub.4 = f32[1,128,2048]{2,1,0:T(8,128)} subtract(f32[1,128,2048]{2,1,0:T(8,128)S(1)} %convert_add_fusion, f32[1,128,2048]{2,1,0:T(8,128)} %reshape.40) | non-fusion elementwise | flops 262144 | bytes 3145728 | tf_op jit(solution)/shard_map/sub | solution.py:42
  15.9 39.3 %psum.14 = f32[2,8,32,8]{2,3,1,0:T(8,128)S(1)} all-reduce(f32[2,8,32,8]{2,3,1,0:T(8,128)S(1)} %convolution_bitcast_fusion.1), channel_id=1, replica_groups=mesh['dp'=8,'tensor'=4] {'dp'}, use_global_device_ids=true, to_apply=%region_0.1 | all-reduce | flops 4096 | bytes 32768 | tf_op jit(solution)/shard_map/psum | solution.py:44
  55.2 0.6 fusion.6
  55.8 4.1 %multiply_reduce_fusion = (f32[]{:T(128)}, f32[2,32,64,64]{3,2,1,0:T(8,128)S(1)}) fusion(f32[8]{0:T(128)S(1)} %compare_select_fusion, f32[64]{0:T(128)S(1)} %add_multiply_fusion, f32[2,32,8,64]{3,1,2,0:T(8,128)S(1)} %fusion.6), kind=kOutput, calls=%fused_computation.3 | convolution fusion | flops 25691648 | bytes 1179940 | tf_op jit(solution)/shard_map/ka,rkcl,lb->racb/dot_general | solution.py:33
  59.9 6.3 %psum.15 = f32[]{:T(128)} all-reduce(f32[]{:T(128)} %get-tuple-element.2), channel_id=1, replica_groups=mesh['dp'=8,'tensor'=4] {'tensor'}, use_global_device_ids=true, to_apply=%region_2.3 | all-reduce | flops 1 | bytes 8 | tf_op jit(solution)/shard_map/psum | solution.py:46
  66.8 0.2 divide_bitcast_fusion
  67.1 1.2 %copy.5 = f32[2,64,32,64]{3,2,1,0:T(8,128)S(1)} copy(f32[2,64,32,64]{3,1,2,0:T(8,128)S(1)} %divide_bitcast_fusion) | data formatting | bytes 2097152 | tf_op jit(solution)/shard_map/div | solution.py:48
  68.3 1.6 %div.37 = f32[128,2048]{1,0:T(8,128)} reshape(f32[2,64,32,64]{3,2,1,0:T(8,128)S(1)} %copy.5) | data formatting | bytes 2097152 | tf_op jit(solution)/shard_map/div | solution.py:48
  (2 shorter events, 0.0 us)
where the time goes:
time: 70.2 us; the launch traced here: 69.9 us
  blocking collectives  45.5 us (65%)
  matrix products  12.4 us (18%)
  local copies, waits for them, and re-layouts  6.51 us (9%)
  other arithmetic  4.07 us (6%)
  between operations  1.4 us (2%)
    psum x1, blocking collectives, body(): total = lax.psum(flat, 'dp')  39.3 us
    dot_general x4, matrix products, decode(): jnp.einsum('ka,rkcl,lb->racb', basis, coeffs, basis, precision=lax.Precis...  8.87 us
    psum x1, blocking collectives, body(): squares = lax.psum(jnp.sum(decoded * decoded), 'tensor')  6.27 us
    dot_general x2, matrix products, encode(): jnp.einsum('ka,racb,lb->rkcl', basis, tiles, basis, precision=lax.Precisi...  3.53 us
    div x2, local copies, waits for them, and re-layouts, body(): return (new_momentum, decoded / scale)  2.84 us
    sub x1, other arithmetic, body(): new_momentum = (accum - decode(coeffs, basis))[None]  2.31 us
    reshape x1, local copies, waits for them, and re-layouts, decode(): return tiles.reshape(nrb * BLOCK, ncb * BLOCK)  1.62 us
    add x1, other arithmetic, body(): accum = momentum_decay * momentum[0] + gradient[0].astype(jnp.float32)  1.51 us

commit v1 on v0

v1 whole, which is shorter than its diff:
```python
import functools

import jax
import jax.numpy as jnp
import ml_dtypes
import numpy as np
from jax import lax
from jax.experimental import pallas as pl
from jax.experimental.pallas import tpu as pltpu
from jax.sharding import PartitionSpec as P

BLOCK = 64
KEEP = 8
TILE = 256
LANES = 128
GROUP = TILE // BLOCK * KEEP

momentum_decay = 0.999

BF16 = jnp.bfloat16
F32 = jnp.float32
MESH = pl.DeviceIdType.MESH


def low_basis():
    freq = np.arange(KEEP, dtype=np.float64)[:, None]
    place = np.arange(BLOCK, dtype=np.float64)[None, :]
    table = np.cos(np.pi * (2.0 * place + 1.0) * freq / (2.0 * BLOCK))
    factor = np.where(freq == 0.0, np.sqrt(1.0 / BLOCK), np.sqrt(2.0 / BLOCK))
    return (table * factor).astype(np.float32)


def halves(table):
    high = table.astype(ml_dtypes.bfloat16)
    low = (table - high.astype(np.float32)).astype(ml_dtypes.bfloat16)
    return high, low


def tables(rows):
    basis = low_basis()
    down = np.kron(np.eye(rows // BLOCK, dtype=np.float32), basis)
    across = np.kron(np.eye(TILE // BLOCK, dtype=np.float32), basis)
    dh, dl = halves(down)
    ah, al = halves(across)
    row_enc = np.concatenate([np.concatenate([dh, dh], 1), np.concatenate([dl, dl], 1)], 0)
    col_enc = np.zeros((TILE, 2 * LANES), ml_dtypes.bfloat16)
    col_enc[:, :GROUP] = ah.T
    col_enc[:, LANES:LANES + GROUP] = al.T
    col_dec = np.concatenate([ah, ah, al, al], 0)
    row_dec = np.concatenate([dh.T, dl.T, dh.T, dl.T], 1)
    parts = (row_enc, col_enc, col_dec, row_dec)
    table = np.zeros((sum(p.shape[0] for p in parts), TILE), np.float32)
    spans, at = [], 0
    for p in parts:
        table[at:at + p.shape[0], :p.shape[1]] = p.astype(np.float32)
        spans.append((at, *p.shape))
        at += p.shape[0]
    return table, spans


def split(value):
    high = value.astype(BF16)
    return high, (value - high.astype(F32)).astype(BF16)


def dot(left, right):
    return jnp.dot(left, right, preferred_element_type=F32)


def spread(coeffs, t):
    half, j = divmod(t * GROUP, LANES)
    j //= GROUP
    part = coeffs[:, half * LANES:(half + 1) * LANES]
    group = lax.broadcasted_iota(jnp.int32, part.shape, 1) // GROUP
    part = jnp.where(group == j, part, 0.0)
    part = part + pltpu.roll(part, 2 * GROUP, 1)
    part = part + pltpu.roll(part, GROUP, 1)
    high = part.astype(BF16).astype(F32)
    return jnp.where(group % 2 == 0, high, part - high).astype(BF16)


def decode_tiles(coeffs, tiles, col_dec, row_dec, emit):
    kr = coeffs.shape[0]
    left = jnp.concatenate([spread(coeffs, t) for t in range(tiles)], 0)
    wide = dot(left, col_dec)
    for t in range(tiles):
        high, low = split(wide[t * kr:(t + 1) * kr])
        emit(t, dot(row_dec, jnp.concatenate([high, high, low, low], 0)))


def exchange_kernel(n_dp, n_tp, chunks, spans, g_hbm, m_hbm, table_hbm,
                    nm_ref, out_ref, col_dec_ref, row_dec_ref, g_buf, table_buf, mine, slots, sq_slots,
                    load_sems, table_sem, send_sems, recv_sems, sq_send, sq_recv):
    rows, cols = nm_ref.shape
    kr = rows // BLOCK * KEEP
    tiles = cols // TILE
    step = cols // chunks
    table_load = pltpu.make_async_copy(table_hbm, table_buf, table_sem)
    table_load.start()
    loads = []
    for c in range(chunks):
        at = pl.ds(c * step, step)
        loads.append((
            pltpu.make_async_copy(m_hbm.at[0, :, at], nm_ref.at[:, at], load_sems.at[0, c]),
            pltpu.make_async_copy(g_hbm.at[0, :, at], g_buf.at[:, at], load_sems.at[1, c]),
        ))
        for load in loads[-1]:
            load.start()

    me = lax.axis_index("dp")
    col = lax.axis_index("tensor")
    barrier = pltpu.get_barrier_semaphore()
    for d in range(1, n_dp):
        pl.semaphore_signal(barrier, inc=1, device_id=(lax.rem(me + d, n_dp), col),
                            device_id_type=MESH)
    for d in range(1, n_tp):
        pl.semaphore_signal(barrier, inc=1, device_id=(me, lax.rem(col + d, n_tp)),
                            device_id_type=MESH)

    table_load.wait()
    row_enc, col_enc, col_dec, row_dec = (
        table_buf[at:at + r, :].astype(BF16)[:, :c] for at, r, c in spans)
    col_dec_ref[...] = col_dec
    row_dec_ref[...] = row_dec
    rows_done = []
    for t in range(tiles):
        if t * TILE % step == 0:
            for load in loads[t * TILE // step]:
                load.wait()
        at = pl.ds(t * TILE, TILE)
        accum = momentum_decay * nm_ref[:, at] + g_buf[:, at].astype(F32)
        nm_ref[:, at] = accum
        both = dot(row_enc, jnp.concatenate(split(accum), 0))
        rows_done.extend(split(both[:kr] + both[kr:]))
    both = dot(jnp.concatenate(rows_done, 0), col_enc)
    both = both[:, :LANES] + both[:, LANES:]
    per = LANES // GROUP
    parts = []
    for h in range(tiles // per):
        acc = None
        for j in range(per):
            base = (h * per + j) * 2 * kr
            part = both[base:base + kr] + both[base + kr:base + 2 * kr]
            if j:
                part = pltpu.roll(part, GROUP * j, 1)
            acc = part if acc is None else acc + part
        parts.append(acc)
    coeffs = jnp.concatenate(parts, 1)
    mine[...] = coeffs

    pl.semaphore_wait(barrier, n_dp - 1 + n_tp - 1)
    copies = []
    for d in range(1, n_dp):
        copy = pltpu.make_async_remote_copy(
            src_ref=mine, dst_ref=slots.at[me],
            send_sem=send_sems.at[d], recv_sem=recv_sems.at[d],
            device_id=(lax.rem(me + d, n_dp), col), device_id_type=MESH)
        copy.start()
        copies.append(copy)
    slots[me] = coeffs

    def remove(t, tile):
        at = pl.ds(t * TILE, TILE)
        nm_ref[:, at] = nm_ref[:, at] - tile

    decode_tiles(coeffs, tiles, col_dec, row_dec, remove)

    for copy in copies:
        copy.wait()
    total = slots[0]
    for d in range(1, n_dp):
        total = total + slots[d]
    square = total * total
    sq = None
    for r in range(0, kr, 8):
        for c in range(0, cols // KEEP, LANES):
            part = square[r:r + 8, c:c + LANES]
            sq = part if sq is None else sq + part
    sq_slots[col] = sq
    copies = []
    for d in range(1, n_tp):
        copy = pltpu.make_async_remote_copy(
            src_ref=sq_slots.at[col], dst_ref=sq_slots.at[col],
            send_sem=sq_send.at[d], recv_sem=sq_recv.at[d],
            device_id=(me, lax.rem(col + d, n_tp)), device_id_type=MESH)
        copy.start()
        copies.append(copy)
    for copy in copies:
        copy.wait()
    squares = sq_slots[0]
    for d in range(1, n_tp):
        squares = squares + sq_slots[d]
    squares = jnp.sum(jnp.sum(squares, 0, keepdims=True), 1, keepdims=True)
    scale = jnp.sqrt(squares / float(rows * cols * n_tp) + 1e-06)
    out_ref[...] = total / scale


def write_kernel(nm_ref, total_ref, col_dec, row_dec, nm_out, up_out, buf, sems):
    rows, cols = nm_ref.shape
    tiles = cols // TILE
    first = pltpu.make_async_copy(nm_ref, nm_out.at[0], sems.at[tiles])
    first.start()
    copies = []

    def store(t, tile):
        at = pl.ds(t * TILE, TILE)
        buf[:, at] = tile
        copy = pltpu.make_async_copy(buf.at[:, at], up_out.at[:, at], sems.at[t])
        copy.start()
        copies.append(copy)

    decode_tiles(total_ref[...], tiles, col_dec[...], row_dec[...], store)
    for copy in copies:
        copy.wait()
    first.wait()


def body(n_dp, n_tp, gradient, momentum):
    _, rows, cols = momentum.shape
    kr = rows // BLOCK * KEEP
    kc = cols // KEEP
    chunks = 4
    table, spans = tables(rows)
    vmem = pl.BlockSpec(memory_space=pltpu.VMEM)
    hbm = pl.BlockSpec(memory_space=pltpu.HBM)
    nm, total, col_dec, row_dec = pl.pallas_call(
        functools.partial(exchange_kernel, n_dp, n_tp, chunks, spans),
        name="encode_exchange",
        out_shape=(jax.ShapeDtypeStruct((rows, cols), F32), jax.ShapeDtypeStruct((kr, kc), F32),
                   jax.ShapeDtypeStruct(spans[2][1:], BF16), jax.ShapeDtypeStruct(spans[3][1:], BF16)),
        in_specs=[hbm, hbm, hbm],
        out_specs=(vmem,) * 4,
        scratch_shapes=[
            pltpu.VMEM((rows, cols), BF16),
            pltpu.VMEM(table.shape, F32),
            pltpu.VMEM((kr, kc), F32),
            pltpu.VMEM((n_dp, kr, kc), F32),
            pltpu.VMEM((n_tp, 8, LANES), F32),
            pltpu.SemaphoreType.DMA((2, chunks)),
            pltpu.SemaphoreType.DMA,
            pltpu.SemaphoreType.DMA((n_dp,)),
            pltpu.SemaphoreType.DMA((n_dp,)),
            pltpu.SemaphoreType.DMA((n_tp,)),
            pltpu.SemaphoreType.DMA((n_tp,)),
        ],
        compiler_params=pltpu.CompilerParams(
            collective_id=0, has_side_effects=True, vmem_limit_bytes=16 * 2**20),
    )(gradient, momentum, jnp.asarray(table))
    return pl.pallas_call(
        write_kernel,
        name="decode_write",
        out_shape=(jax.ShapeDtypeStruct((1, rows, cols), F32), jax.ShapeDtypeStruct((rows, cols), F32)),
        in_specs=[vmem] * 4,
        out_specs=(hbm, hbm),
        scratch_shapes=[
            pltpu.VMEM((rows, cols), F32),
            pltpu.SemaphoreType.DMA((cols // TILE + 1,)),
        ],
        compiler_params=pltpu.CompilerParams(vmem_limit_bytes=16 * 2**20),
    )(nm, total, col_dec, row_dec)


def solution(mesh):
    placed = (P("dp", None, "tensor"), P("dp", None, "tensor"))
    return jax.shard_map(
        functools.partial(body, mesh.shape["dp"], mesh.shape["tensor"]),
        mesh=mesh,
        in_specs=placed,
        out_specs=(P("dp", None, "tensor"), P(None, "tensor")),
        check_vma=False,
    )
```

time: 70.2 us -> 18.9 us (0.27)
  blocking collectives: 45.5 us -> 0 us
  Pallas kernels: 0 us -> 14.7 us
  matrix products: 12.4 us -> 0 us
  other arithmetic: 4.07 us -> 0 us
  local copies, waits for them, and re-layouts: 6.51 us -> 3.31 us
  between operations: 1.4 us -> 0.65 us
    psum x2 -> x0, blocking collectives: 45.5 us -> none  [the longest x1 39.3 us: body(): total = lax.psum(flat, 'dp')]
    pallas_call x0 -> x2, Pallas kernels: none -> 14.7 us  [the longest x1 13.3 us: body(): pl.pallas_call(functools.partial(exchange_kernel, n_dp, n_tp, chunks, spa...]
    dot_general x6 -> x0, matrix products: 12.4 us -> none  [the longest x4 8.87 us: decode(): jnp.einsum('ka,rkcl,lb->racb', basis, coeffs, basis, precision=lax.Precis...]
    unnamed x0 -> x6, local copies, waits for them, and re-layouts: none -> 3.31 us
    div x2 -> x0, local copies, waits for them, and re-layouts: 2.84 us -> none  [body(): return (new_momentum, decoded / scale)]
    sub x1 -> x0, other arithmetic: 2.31 us -> none  [body(): new_momentum = (accum - decode(coeffs, basis))[None]]
    reshape x1 -> x0, local copies, waits for them, and re-layouts: 1.62 us -> none  [decode(): return tiles.reshape(nrb * BLOCK, ncb * BLOCK)]
    add x1 -> x0, other arithmetic: 1.51 us -> none  [body(): accum = momentum_decay * momentum[0] + gradient[0].astype(jnp.float32)]
where the time goes in v1:
time: 18.9 us; the launch traced here: 18.7 us
  Pallas kernels  14.7 us (78%)
  local copies, waits for them, and re-layouts  3.31 us (18%)
  between operations  0.65 us (3%)
    pallas_call x1, Pallas kernels, body(): pl.pallas_call(functools.partial(exchange_kernel, n_dp, n_tp, chunks, spa...  13.3 us
    unnamed x6, local copies, waits for them, and re-layouts  3.31 us
    pallas_call x1, Pallas kernels, body(): pl.pallas_call(write_kernel, name='decode_write', out_shape=(jax.ShapeDty...  1.47 us

profile of v1, /device:TPU:0, one launch (start us, length us, event | category | flops | bytes accessed | tf_op | source)
XLA Modules:
  0.0 18.7 jit_solution(305866486876041859)
XLA Ops:
  0.6 0.0 copy-start
  0.6 1.2 %copy-done = f32[1,128,2048]{2,1,0:T(8,128)S(1)} copy-done((f32[1,128,2048]{2,1,0:T(8,128)S(1)}, f32[1,128,2048]{2,1,0:T(8,128)}, u32[]{:S(2)}) %copy-start) | copy-done | bytes 1048600
  1.9 0.0 copy-start.1
  1.9 1.1 %copy-done.1 = f32[544,256]{1,0:T(8,128)S(1)} copy-done((f32[544,256]{1,0:T(8,128)S(1)}, f32[544,256]{1,0:T(8,128)}, u32[]{:S(2)}) %copy-start.1) | copy-done | bytes 557080
  2.9 0.0 copy-start.2
  2.9 1.0 %copy-done.2 = bf16[1,128,2048]{2,1,0:T(8,128)(2,1)S(1)} copy-done((bf16[1,128,2048]{2,1,0:T(8,128)(2,1)S(1)}, bf16[1,128,2048]{2,1,0:T(8,128)(2,1)}, u32[]{:S(2)}) %copy-start.2) | copy-done | bytes 524312
  4.0 13.3 %encode_exchange.1 = (f32[128,2048]{1,0:T(8,128)S(1)}, f32[16,256]{1,0:T(8,128)S(1)}, bf16[128,256]{1,0:T(8,128)(2,1)S(1)}, bf16[128,64]{1,0:T(8,128)(2,1)S(1)}) custom-call(bf16[1,128,2048]{2,1,0:T(8,128)(2,1)S(1)} %copy-done.2, f32[1,128,2048]{2,1,0:T(8,128)S(1)} %copy-done, f32[544,256]{1,0:T(8,128)S(1)} %copy-done.1), custom_call_target="tpu_custom_call" | custom-call | tf_op jit(solution)/shard_map/encode_exchange/pallas_call | solution.py:226
  17.2 1.5 %decode_write.1 = (f32[1,128,2048]{2,1,0:T(8,128)}, f32[128,2048]{1,0:T(8,128)}) custom-call(f32[128,2048]{1,0:T(8,128)S(1)} %get-tuple-element.6.nm_ref, f32[16,256]{1,0:T(8,128)S(1)} %get-tuple-element.7.total_ref, bf16[128,256]{1,0:T(8,128)(2,1)S(1)} %get-tuple-element.8.col_dec, bf16[128,64]{1,0:T(8,128)(2,1)S(1)} %get-tuple-element.9.row_dec), custom_call_target="tpu_custom_call" | custom-call | tf_op jit(solution)/shard_map/decode_write/pallas_call | solution.py:249
Async XLA Ops:
  0.6 1.2 %copy-start = (f32[1,128,2048]{2,1,0:T(8,128)S(1)}, f32[1,128,2048]{2,1,0:T(8,128)}, u32[]{:S(2)}) copy-start(f32[1,128,2048]{2,1,0:T(8,128)} %m_hbm.1) | copy-start | bytes 3145732
  1.9 1.1 %copy-start.1 = (f32[544,256]{1,0:T(8,128)S(1)}, f32[544,256]{1,0:T(8,128)}, u32[]{:S(2)}) copy-start(f32[544,256]{1,0:T(8,128)} %constant.2.clone.table_hbm) | copy-start | bytes 1671172
  2.9 1.0 %copy-start.2 = (bf16[1,128,2048]{2,1,0:T(8,128)(2,1)S(1)}, bf16[1,128,2048]{2,1,0:T(8,128)(2,1)}, u32[]{:S(2)}) copy-start(bf16[1,128,2048]{2,1,0:T(8,128)(2,1)} %g_hbm.1) | copy-start | bytes 1572868

commit v2 on v1

--- a/solution.py
+++ b/solution.py
@@ -166,7 +166,7 @@
     decode_tiles(coeffs, tiles, col_dec, row_dec, remove)
 
     for copy in copies:
-        copy.wait()
+        copy.wait_recv()
     total = slots[0]
     for d in range(1, n_dp):
         total = total + slots[d]
@@ -177,22 +177,24 @@
             part = square[r:r + 8, c:c + LANES]
             sq = part if sq is None else sq + part
     sq_slots[col] = sq
-    copies = []
+    sq_copies = []
     for d in range(1, n_tp):
         copy = pltpu.make_async_remote_copy(
             src_ref=sq_slots.at[col], dst_ref=sq_slots.at[col],
             send_sem=sq_send.at[d], recv_sem=sq_recv.at[d],
             device_id=(me, lax.rem(col + d, n_tp)), device_id_type=MESH)
         copy.start()
-        copies.append(copy)
-    for copy in copies:
-        copy.wait()
+        sq_copies.append(copy)
+    for copy in sq_copies:
+        copy.wait_recv()
     squares = sq_slots[0]
     for d in range(1, n_tp):
         squares = squares + sq_slots[d]
     squares = jnp.sum(jnp.sum(squares, 0, keepdims=True), 1, keepdims=True)
     scale = jnp.sqrt(squares / float(rows * cols * n_tp) + 1e-06)
-    out_ref[...] = total / scale
+    out_ref[...] = total * (1.0 / scale)
+    for copy in copies + sq_copies:
+        copy.wait_send()
 
 
 def write_kernel(nm_ref, total_ref, col_dec, row_dec, nm_out, up_out, buf, sems):
@@ -219,7 +221,7 @@
     _, rows, cols = momentum.shape
     kr = rows // BLOCK * KEEP
     kc = cols // KEEP
-    chunks = 4
+    chunks = 2
     table, spans = tables(rows)
     vmem = pl.BlockSpec(memory_space=pltpu.VMEM)
     hbm = pl.BlockSpec(memory_space=pltpu.HBM)
@@ -245,7 +247,8 @@
         ],
         compiler_params=pltpu.CompilerParams(
             collective_id=0, has_side_effects=True, vmem_limit_bytes=16 * 2**20),
-    )(gradient, momentum, jnp.asarray(table))
+    )(*(pltpu.with_memory_space_constraint(a, pltpu.HBM)
+        for a in (gradient, momentum, jnp.asarray(table))))
     return pl.pallas_call(
         write_kernel,
         name="decode_write",

time: 18.9 us -> 16.1 us (0.85)
  local copies, waits for them, and re-layouts: 3.31 us -> 0 us
  Pallas kernels: 14.7 us -> 15.3 us
    unnamed x6 -> x0, local copies, waits for them, and re-layouts: 3.31 us -> none
    pallas_call x1, Pallas kernels: 13.3 us -> 13.8 us  [body(): pl.pallas_call(functools.partial(exchange_kernel, n_dp, n_tp, chunks, spa...]
where the time goes in v2:
time: 16.1 us; the launch traced here: 15.9 us
  Pallas kernels  15.3 us (95%)
  between operations  0.64 us (4%)
    pallas_call x1, Pallas kernels, body(): pl.pallas_call(functools.partial(exchange_kernel, n_dp, n_tp, chunks, spa...  13.8 us
    pallas_call x1, Pallas kernels, body(): pl.pallas_call(write_kernel, name='decode_write', out_shape=(jax.ShapeDty...  1.47 us

profile of v2, /device:TPU:0, one launch (start us, length us, event | category | flops | bytes accessed | tf_op | source)
XLA Modules:
  0.0 15.9 jit_solution(3852611390651318610)
XLA Ops:
  0.6 13.8 %encode_exchange.1 = (f32[128,2048]{1,0:T(8,128)S(1)}, f32[16,256]{1,0:T(8,128)S(1)}, bf16[128,256]{1,0:T(8,128)(2,1)S(1)}, bf16[128,64]{1,0:T(8,128)(2,1)S(1)}) custom-call(bf16[1,128,2048]{2,1,0:T(8,128)(2,1)} %g_hbm.1, f32[1,128,2048]{2,1,0:T(8,128)} %m_hbm.1, f32[544,256]{1,0:T(8,128)} %constant.2.clone.table_hbm), custom_call_target="tpu_custom_call" | custom-call | tf_op jit(solution)/shard_map/encode_exchange/pallas_call | solution.py:228
  14.5 1.5 %decode_write.1 = (f32[1,128,2048]{2,1,0:T(8,128)}, f32[128,2048]{1,0:T(8,128)}) custom-call(f32[128,2048]{1,0:T(8,128)S(1)} %get-tuple-element.6.nm_ref, f32[16,256]{1,0:T(8,128)S(1)} %get-tuple-element.7.total_ref, bf16[128,256]{1,0:T(8,128)(2,1)S(1)} %get-tuple-element.8.col_dec, bf16[128,64]{1,0:T(8,128)(2,1)S(1)} %get-tuple-element.9.row_dec), custom_call_target="tpu_custom_call" | custom-call | tf_op jit(solution)/shard_map/decode_write/pallas_call | solution.py:252

commit v3 on v2

--- a/solution.py
+++ b/solution.py
@@ -118,10 +118,7 @@
                             device_id_type=MESH)
 
     table_load.wait()
-    row_enc, col_enc, col_dec, row_dec = (
-        table_buf[at:at + r, :].astype(BF16)[:, :c] for at, r, c in spans)
-    col_dec_ref[...] = col_dec
-    row_dec_ref[...] = row_dec
+    row_enc, col_enc = (table_buf[at:at + r, :].astype(BF16)[:, :c] for at, r, c in spans[:2])
     rows_done = []
     for t in range(tiles):
         if t * TILE % step == 0:
@@ -158,6 +155,9 @@
         copy.start()
         copies.append(copy)
     slots[me] = coeffs
+    col_dec, row_dec = (table_buf[at:at + r, :].astype(BF16)[:, :c] for at, r, c in spans[2:])
+    col_dec_ref[...] = col_dec
+    row_dec_ref[...] = row_dec
 
     def remove(t, tile):
         at = pl.ds(t * TILE, TILE)

time: 16.1 us -> 15.8 us (0.981)
  Pallas kernels: 15.3 us -> 15 us
    pallas_call x1, Pallas kernels: 13.8 us -> 13.5 us  [body(): pl.pallas_call(functools.partial(exchange_kernel, n_dp, n_tp, chunks, spa...]
where the time goes in v3:
time: 15.8 us; the launch traced here: 15.6 us
  Pallas kernels  15 us (95%)
  between operations  0.64 us (4%)
    pallas_call x1, Pallas kernels, body(): pl.pallas_call(functools.partial(exchange_kernel, n_dp, n_tp, chunks, spa...  13.5 us
    pallas_call x1, Pallas kernels, body(): pl.pallas_call(write_kernel, name='decode_write', out_shape=(jax.ShapeDty...  1.47 us

profile of v3, /device:TPU:0, one launch (start us, length us, event | category | flops | bytes accessed | tf_op | source)
XLA Modules:
  0.0 15.6 jit_solution(11447340440167816187)
XLA Ops:
  0.6 13.5 %encode_exchange.1 = (f32[128,2048]{1,0:T(8,128)S(1)}, f32[16,256]{1,0:T(8,128)S(1)}, bf16[128,256]{1,0:T(8,128)(2,1)S(1)}, bf16[128,64]{1,0:T(8,128)(2,1)S(1)}) custom-call(bf16[1,128,2048]{2,1,0:T(8,128)(2,1)} %g_hbm.1, f32[1,128,2048]{2,1,0:T(8,128)} %m_hbm.1, f32[544,256]{1,0:T(8,128)} %constant.2.clone.table_hbm), custom_call_target="tpu_custom_call" | custom-call | tf_op jit(solution)/shard_map/encode_exchange/pallas_call | solution.py:228
  14.2 1.5 %decode_write.1 = (f32[1,128,2048]{2,1,0:T(8,128)}, f32[128,2048]{1,0:T(8,128)}) custom-call(f32[128,2048]{1,0:T(8,128)S(1)} %get-tuple-element.6.nm_ref, f32[16,256]{1,0:T(8,128)S(1)} %get-tuple-element.7.total_ref, bf16[128,256]{1,0:T(8,128)(2,1)S(1)} %get-tuple-element.8.col_dec, bf16[128,64]{1,0:T(8,128)(2,1)S(1)} %get-tuple-element.9.row_dec), custom_call_target="tpu_custom_call" | custom-call | tf_op jit(solution)/shard_map/decode_write/pallas_call | solution.py:252

commit v4 on v3

--- a/solution.py
+++ b/solution.py
@@ -90,13 +90,16 @@
 
 def exchange_kernel(n_dp, n_tp, chunks, spans, g_hbm, m_hbm, table_hbm,
                     nm_ref, out_ref, col_dec_ref, row_dec_ref, g_buf, table_buf, mine, slots, sq_slots,
-                    load_sems, table_sem, send_sems, recv_sems, sq_send, sq_recv):
+                    load_sems, table_sems, send_sems, recv_sems, sq_send, sq_recv):
     rows, cols = nm_ref.shape
     kr = rows // BLOCK * KEEP
     tiles = cols // TILE
     step = cols // chunks
-    table_load = pltpu.make_async_copy(table_hbm, table_buf, table_sem)
-    table_load.start()
+    first = spans[0][1]
+    table_loads = [
+        pltpu.make_async_copy(table_hbm.at[at], table_buf.at[at], table_sems.at[i])
+        for i, at in enumerate((pl.ds(0, first), pl.ds(first, table_buf.shape[0] - first)))]
+    table_loads[0].start()
     loads = []
     for c in range(chunks):
         at = pl.ds(c * step, step)
@@ -107,8 +110,11 @@
         for load in loads[-1]:
             load.start()
 
+    table_loads[1].start()
+
     me = lax.axis_index("dp")
     col = lax.axis_index("tensor")
+    upper = (2 * me) // n_dp
     barrier = pltpu.get_barrier_semaphore()
     for d in range(1, n_dp):
         pl.semaphore_signal(barrier, inc=1, device_id=(lax.rem(me + d, n_dp), col),
@@ -117,8 +123,12 @@
         pl.semaphore_signal(barrier, inc=1, device_id=(me, lax.rem(col + d, n_tp)),
                             device_id_type=MESH)
 
-    table_load.wait()
-    row_enc, col_enc = (table_buf[at:at + r, :].astype(BF16)[:, :c] for at, r, c in spans[:2])
+    def table(i):
+        at, r, c = spans[i]
+        return table_buf[at:at + r, :].astype(BF16)[:, :c]
+
+    table_loads[0].wait()
+    row_enc = table(0)
     rows_done = []
     for t in range(tiles):
         if t * TILE % step == 0:
@@ -129,7 +139,8 @@
         nm_ref[:, at] = accum
         both = dot(row_enc, jnp.concatenate(split(accum), 0))
         rows_done.extend(split(both[:kr] + both[kr:]))
-    both = dot(jnp.concatenate(rows_done, 0), col_enc)
+    table_loads[1].wait()
+    both = dot(jnp.concatenate(rows_done, 0), table(1))
     both = both[:, :LANES] + both[:, LANES:]
     per = LANES // GROUP
     parts = []
@@ -147,15 +158,16 @@
 
     pl.semaphore_wait(barrier, n_dp - 1 + n_tp - 1)
     copies = []
-    for d in range(1, n_dp):
+    for k in range(1, n_dp):
+        d = upper * k + (1 - upper) * (n_dp - k)
         copy = pltpu.make_async_remote_copy(
             src_ref=mine, dst_ref=slots.at[me],
-            send_sem=send_sems.at[d], recv_sem=recv_sems.at[d],
+            send_sem=send_sems.at[k], recv_sem=recv_sems.at[d],
             device_id=(lax.rem(me + d, n_dp), col), device_id_type=MESH)
         copy.start()
         copies.append(copy)
     slots[me] = coeffs
-    col_dec, row_dec = (table_buf[at:at + r, :].astype(BF16)[:, :c] for at, r, c in spans[2:])
+    col_dec, row_dec = table(2), table(3)
     col_dec_ref[...] = col_dec
     row_dec_ref[...] = row_dec
 
@@ -165,8 +177,11 @@
 
     decode_tiles(coeffs, tiles, col_dec, row_dec, remove)
 
-    for copy in copies:
-        copy.wait_recv()
+    for d in range(1, n_dp):
+        pltpu.make_async_remote_copy(
+            src_ref=mine, dst_ref=slots.at[lax.rem(me + n_dp - d, n_dp)],
+            send_sem=send_sems.at[d], recv_sem=recv_sems.at[d],
+            device_id=(lax.rem(me + d, n_dp), col), device_id_type=MESH).wait_recv()
     total = slots[0]
     for d in range(1, n_dp):
         total = total + slots[d]
@@ -178,7 +193,7 @@
             sq = part if sq is None else sq + part
     sq_slots[col] = sq
     sq_copies = []
-    for d in range(1, n_tp):
+    for d in sorted(range(1, n_tp), key=lambda d: d % 2):
         copy = pltpu.make_async_remote_copy(
             src_ref=sq_slots.at[col], dst_ref=sq_slots.at[col],
             send_sem=sq_send.at[d], recv_sem=sq_recv.at[d],
@@ -239,7 +254,7 @@
             pltpu.VMEM((n_dp, kr, kc), F32),
             pltpu.VMEM((n_tp, 8, LANES), F32),
             pltpu.SemaphoreType.DMA((2, chunks)),
-            pltpu.SemaphoreType.DMA,
+            pltpu.SemaphoreType.DMA((2,)),
             pltpu.SemaphoreType.DMA((n_dp,)),
             pltpu.SemaphoreType.DMA((n_dp,)),
             pltpu.SemaphoreType.DMA((n_tp,)),

time: 15.8 us -> 15.5 us (0.981)
  Pallas kernels: 15 us -> 14.7 us
    pallas_call x1, Pallas kernels: 13.5 us -> 13.3 us  [body(): pl.pallas_call(functools.partial(exchange_kernel, n_dp, n_tp, chunks, spa...]
where the time goes in v4:
time: 15.5 us; the launch traced here: 15.4 us
  Pallas kernels  14.7 us (95%)
  between operations  0.64 us (4%)
    pallas_call x1, Pallas kernels, body(): pl.pallas_call(functools.partial(exchange_kernel, n_dp, n_tp, chunks, spa...  13.3 us
    pallas_call x1, Pallas kernels, body(): pl.pallas_call(write_kernel, name='decode_write', out_shape=(jax.ShapeDty...  1.47 us

profile of v4, /device:TPU:0, one launch (start us, length us, event | category | flops | bytes accessed | tf_op | source)
XLA Modules:
  0.0 15.4 jit_solution(18025981185970806162)
XLA Ops:
  0.6 13.3 %encode_exchange.1 = (f32[128,2048]{1,0:T(8,128)S(1)}, f32[16,256]{1,0:T(8,128)S(1)}, bf16[128,256]{1,0:T(8,128)(2,1)S(1)}, bf16[128,64]{1,0:T(8,128)(2,1)S(1)}) custom-call(bf16[1,128,2048]{2,1,0:T(8,128)(2,1)} %g_hbm.1, f32[1,128,2048]{2,1,0:T(8,128)} %m_hbm.1, f32[544,256]{1,0:T(8,128)} %constant.2.clone.table_hbm), custom_call_target="tpu_custom_call" | custom-call | tf_op jit(solution)/shard_map/encode_exchange/pallas_call | solution.py:243
  13.9 1.5 %decode_write.1 = (f32[1,128,2048]{2,1,0:T(8,128)}, f32[128,2048]{1,0:T(8,128)}) custom-call(f32[128,2048]{1,0:T(8,128)S(1)} %get-tuple-element.6.nm_ref, f32[16,256]{1,0:T(8,128)S(1)} %get-tuple-element.7.total_ref, bf16[128,256]{1,0:T(8,128)(2,1)S(1)} %get-tuple-element.8.col_dec, bf16[128,64]{1,0:T(8,128)(2,1)S(1)} %get-tuple-element.9.row_dec), custom_call_target="tpu_custom_call" | custom-call | tf_op jit(solution)/shard_map/decode_write/pallas_call | solution.py:267

commit v5 on v4

--- a/solution.py
+++ b/solution.py
@@ -110,18 +110,19 @@
         for load in loads[-1]:
             load.start()
 
-    table_loads[1].start()
-
     me = lax.axis_index("dp")
     col = lax.axis_index("tensor")
     upper = (2 * me) // n_dp
     barrier = pltpu.get_barrier_semaphore()
-    for d in range(1, n_dp):
+    for k in range(1, n_dp):
+        d = upper * k + (1 - upper) * (n_dp - k)
         pl.semaphore_signal(barrier, inc=1, device_id=(lax.rem(me + d, n_dp), col),
                             device_id_type=MESH)
     for d in range(1, n_tp):
         pl.semaphore_signal(barrier, inc=1, device_id=(me, lax.rem(col + d, n_tp)),
                             device_id_type=MESH)
+
+    table_loads[1].start()
 
     def table(i):
         at, r, c = spans[i]

time: 15.5 us -> 15.6 us (level)
  no operation moved by 1% of the time
where the time goes in v5:
time: 15.6 us; the launch traced here: 15.4 us
  Pallas kernels  14.8 us (95%)
  between operations  0.64 us (4%)
    pallas_call x1, Pallas kernels, body(): pl.pallas_call(functools.partial(exchange_kernel, n_dp, n_tp, chunks, spa...  13.3 us
    pallas_call x1, Pallas kernels, body(): pl.pallas_call(write_kernel, name='decode_write', out_shape=(jax.ShapeDty...  1.47 us

profile of v5, /device:TPU:0, one launch (start us, length us, event | category | flops | bytes accessed | tf_op | source)
XLA Modules:
  0.0 15.4 jit_solution(14676474431468241280)
XLA Ops:
  0.6 13.3 %encode_exchange.1 = (f32[128,2048]{1,0:T(8,128)S(1)}, f32[16,256]{1,0:T(8,128)S(1)}, bf16[128,256]{1,0:T(8,128)(2,1)S(1)}, bf16[128,64]{1,0:T(8,128)(2,1)S(1)}) custom-call(bf16[1,128,2048]{2,1,0:T(8,128)(2,1)} %g_hbm.1, f32[1,128,2048]{2,1,0:T(8,128)} %m_hbm.1, f32[544,256]{1,0:T(8,128)} %constant.2.clone.table_hbm), custom_call_target="tpu_custom_call" | custom-call | tf_op jit(solution)/shard_map/encode_exchange/pallas_call | solution.py:244
  14.0 1.5 %decode_write.1 = (f32[1,128,2048]{2,1,0:T(8,128)}, f32[128,2048]{1,0:T(8,128)}) custom-call(f32[128,2048]{1,0:T(8,128)S(1)} %get-tuple-element.6.nm_ref, f32[16,256]{1,0:T(8,128)S(1)} %get-tuple-element.7.total_ref, bf16[128,256]{1,0:T(8,128)(2,1)S(1)} %get-tuple-element.8.col_dec, bf16[128,64]{1,0:T(8,128)(2,1)S(1)} %get-tuple-element.9.row_dec), custom_call_target="tpu_custom_call" | custom-call | tf_op jit(solution)/shard_map/decode_write/pallas_call | solution.py:268
